TPU v7x, 256 devices: a whole 4x4x8 slice. The times are simulated.
256 devices in a mesh: dp: 16 (over z, y_lo), land: 16 (over x, y_hi, core).
Axes of the slice: x: 4, y: 4 (y_hi: 2, y_lo: 2; y = y_hi * 2 + y_lo), z: 8, core: 2. Of those that a mesh axis runs over, the one named last changes fastest.
Arguments:
- points: bfloat16 [28672, 768], P(('dp', 'land'))
- landmarks: bfloat16 [32768, 768], P('land')
- factor: bfloat16 [32768, 1024], P('land'), may hold values from -0.03125 to 0.03125
- assignments: int32 [28672], P(('dp', 'land')), may hold values from 0 to 16383, as said below
- owner_map: int32 [16384], replicated, may hold values from 0 to 16383, as said below
- old_centroids: float32 [16384, 1024], P('dp', 'land'), may hold values from -6 to 6
Outputs:
- features: bfloat16 [28672, 1024], P(('dp', 'land'))
- centroids: float32 [16384, 1024], P('dp', 'land')
Inputs may be any that keep to these rules, and one draw needn't show every extreme that they name: A permutation of 0 to 16383: cluster c has row owner_map[c] of the centroid table, and its owner is owner_map[c] // 1024. `assignments`: among the 112 points of one device, exactly 28 lie in clusters of one owner and at most 28 in clusters of any other owner. Every owner has at least one of its clusters that no point names.
All inputs are finite; a program needn't handle non-finite values.
Results may differ from a plain program's by a relative error of at most 0.0064.
Values may be sent and summed in bfloat16 or wider, within the bound.
A program may use at most 64 MiB of HBM per device.

v0:
```python
import math

import jax
import jax.numpy as jnp
from jax import lax
from jax.sharding import PartitionSpec as P


def unit_rows(values):
    widened = values.astype(jnp.float32)
    squared_sum = jnp.sum(widened * widened, axis=1, keepdims=True) + 1e-06
    return (widened * lax.rsqrt(squared_sum)).astype(jnp.bfloat16)


def kernel_block(shard_rows, unit_land, sharpness):
    scores = lax.dot_general(
        shard_rows, unit_land, (((1,), (1,)), ((), ())), preferred_element_type=jnp.float32
    )
    return jnp.exp(sharpness * scores).astype(jnp.bfloat16)


def per_device(points, landmarks, factor, assignments, owner_map, old_centroids):
    sharpness = math.sqrt(points.shape[1])
    unit_land = unit_rows(landmarks)
    unit_points = unit_rows(points)
    row_count = points.shape[0]
    feat_width = factor.shape[1]
    kernel_all = kernel_block(
        lax.all_gather(unit_points, "land", axis=0, tiled=True), unit_land, sharpness
    )
    summed = lax.psum_scatter(
        jnp.dot(kernel_all, factor, preferred_element_type=jnp.float32),
        "land",
        scatter_dimension=0,
        tiled=True,
    )
    features = summed.astype(jnp.bfloat16)
    per_owner = old_centroids.shape[0]
    owners = lax.axis_size("dp")
    capacity = row_count // 4
    slot_ids = jnp.take(owner_map, assignments)
    owner_ids = slot_ids // per_owner
    local_ids = slot_ids % per_owner
    owner_hits = (owner_ids[:, None] == jnp.arange(owners, dtype=jnp.int32)[None, :]).astype(
        jnp.int32
    )
    before = jnp.cumsum(owner_hits, axis=0) - owner_hits
    rank_ids = jnp.sum(before * owner_hits, axis=1)
    positions = owner_ids * capacity + rank_ids
    matches = jnp.arange(owners * capacity, dtype=jnp.int32)[:, None] == positions[None, :]
    packed = jnp.dot(
        matches.astype(jnp.bfloat16), features, preferred_element_type=jnp.float32
    ).astype(jnp.bfloat16)
    packed = packed.reshape(owners, capacity, feat_width)
    labels = jnp.sum(jnp.where(matches, local_ids[None, :] + 1, 0), axis=1) - 1
    labels = labels.reshape(owners, capacity)
    arrived, arrived_labels = (
        lax.all_to_all(packed, "dp", split_axis=0, concat_axis=0, tiled=True),
        lax.all_to_all(labels, "dp", split_axis=0, concat_axis=0, tiled=True),
    )
    flat_rows = arrived.reshape(owners * capacity, feat_width)
    flat_labels = arrived_labels.reshape(owners * capacity)
    assigned = jnp.arange(per_owner, dtype=jnp.int32)[:, None] == flat_labels[None, :]
    part_totals = jnp.dot(
        assigned.astype(jnp.bfloat16), flat_rows, preferred_element_type=jnp.float32
    )
    part_counts = jnp.sum(assigned.astype(jnp.float32), axis=1)
    totals = lax.psum_scatter(
        part_totals.astype(jnp.bfloat16), "land", scatter_dimension=1, tiled=True
    ).astype(jnp.float32)
    counts = lax.psum(part_counts, "land")
    centroids = jnp.where(
        counts[:, None] > 0, totals / jnp.maximum(counts, 1.0)[:, None], old_centroids
    )
    return (features, centroids)


def solution(mesh):
    in_specs = (
        P(("dp", "land"), None),
        P("land", None),
        P("land", None),
        P(("dp", "land")),
        P(),
        P("dp", "land"),
    )
    out_specs = (P(("dp", "land"), None), P("dp", "land"))
    return jax.shard_map(
        per_device, mesh=mesh, in_specs=in_specs, out_specs=out_specs, check_vma=False
    )
```

profile of v0, /device:TPU:11, one launch (start us, length us, event | category | flops | bytes accessed | tf_op | source)
XLA Modules:
  0.0 310.1 jit_solution(15380954529286180247)
XLA Ops:
  7.2 0.0 all-gather.2.cloned.1.call-start
  7.2 1.2 fusion.9
  8.5 1.7 fusion.10
  10.2 0.0 reduce-scatter.3.cloned.1.call-start
  10.2 2.6 fusion
  12.8 56.6 %all-gather.2.cloned.1.call-done = bf16[1792,768]{1,0:T(8,128)(2,1)} async-done(((bf16[112,768]{1,0:T(8,128)(2,1)}), bf16[1792,768]{1,0:T(8,128)(2,1)}) %all-gather.2.cloned.1.call-update) | async-done | bytes 2752528 | tf_op jit(solution)/shard_map/all_gather | solution.py:29
  69.4 19.8 %fusion.4 = f32[1792,1024]{1,0:T(8,128)} fusion(bf16[2048,1024]{1,0:T(8,128)(2,1)} %param.8, bf16[1792,768]{1,0:T(8,128)(2,1)} %all-gather.2.cloned.1.call-done, bf16[2048,768]{1,0:T(8,128)(2,1)S(1)} %copy-done.1, f32[2048]{0:T(1024)S(1)} %add_rsqrt_fusion), kind=kOutput, calls=%fused_computation.6 | convolution fusion | flops 13165395968 | bytes 17440768 | tf_op jit(solution)/shard_map/dot_general | solution.py:32
  89.2 0.0 reduce-scatter.3.cloned.1.call-update
  89.2 0.6 copy-done.4
  89.9 1.1 gather_fusion
  91.1 0.1 fusion.12
  91.2 0.2 reduce_window_sum.11
  91.3 0.2 select_reduce_fusion.1
  91.5 0.2 select_reduce_fusion
  91.7 0.7 sub.18
  92.4 7.9 %all-to-all-start = ((s32[16,1,28]{2,1,0:T(1,128)}), s32[16,1,28]{2,1,0:T(1,128)S(1)}, u32[]{:S(2)}, u32[]{:S(2)}) async-start(s32[16,1,28]{2,1,0:T(1,128)} %sub.18), calls=%async_computation.1 | async-start | bytes 16384 | tf_op jit(solution)/shard_map/all_to_all | solution.py:59
  100.3 88.1 %reduce-scatter.3.cloned.1.call-done = f32[112,1024]{1,0:T(8,128)} async-done(((f32[1792,1024]{1,0:T(8,128)}), f32[112,1024]{1,0:T(8,128)}) %reduce-scatter.3.cloned.1.call-update) | async-done | bytes 458768 | tf_op jit(solution)/shard_map/reduce_scatter | solution.py:31
  188.4 1.0 convert_element_type.40
  189.5 0.4 convolution_convert_fusion.1
  189.9 1.2 reshape.105
  191.0 8.0 %all-to-all-start.1 = ((bf16[16,28,1024]{2,1,0:T(8,128)(2,1)}), bf16[16,28,1024]{2,1,0:T(8,128)(2,1)S(1)}, u32[]{:S(2)}, u32[]{:S(2)}) async-start(bf16[16,28,1024]{2,1,0:T(8,128)(2,1)} %reshape.105), calls=%async_computation.2 | async-start | bytes 2097152 | tf_op jit(solution)/shard_map/all_to_all | solution.py:58
  199.0 0.0 reduce-scatter.5.cloned.1.call-start
  199.1 0.5 broadcast.103
  199.6 0.7 reduce.3
  200.3 0.1 eq.50
  200.4 22.0 %all-to-all-done.1 = bf16[16,28,1024]{2,1,0:T(8,128)(2,1)S(1)} async-done(((bf16[16,28,1024]{2,1,0:T(8,128)(2,1)}), bf16[16,28,1024]{2,1,0:T(8,128)(2,1)S(1)}, u32[]{:S(2)}, u32[]{:S(2)}) %all-to-all-start.1) | async-done | bytes 917536 | tf_op jit(solution)/shard_map/all_to_all | solution.py:58
  222.3 0.2 reshape.106
  222.6 2.8 convolution_convert_fusion
  225.4 0.2 convert_reduce_fusion
  225.6 31.5 %psum.7 = f32[1024]{0:T(1024)S(1)} all-reduce(f32[1024]{0:T(1024)S(1)} %convert_reduce_fusion), channel_id=1, replica_groups=mesh['dp'=16,'land'=16] {'land'}, use_global_device_ids=true, to_apply=%region_7.8 | all-reduce | flops 1024 | bytes 8192 | tf_op jit(solution)/shard_map/psum | solution.py:71
  257.1 44.8 %reduce-scatter.5.cloned.1.call-done = bf16[1024,64]{0,1:T(8,128)(2,1)} async-done(((bf16[1024,1024]{0,1:T(8,128)(2,1)}), bf16[1024,64]{0,1:T(8,128)(2,1)}) %reduce-scatter.5.cloned.1.call-update) | async-done | bytes 131088 | tf_op jit(solution)/shard_map/reduce_scatter | solution.py:68
  301.9 1.6 divide_select_fusion
  (22 shorter events, 0.1 us)
Async XLA Ops:
  7.2 82.7 %copy-start = (s32[16384]{0:T(1024)S(1)}, s32[16384]{0:T(1024)}, u32[]{:S(2)}) copy-start(s32[16384]{0:T(1024)} %param.10) | copy-start | bytes 196612
  7.2 62.2 %copy-start.1 = (bf16[2048,768]{1,0:T(8,128)(2,1)S(1)}, bf16[2048,768]{1,0:T(8,128)(2,1)}, u32[]{:S(2)}) copy-start(bf16[2048,768]{1,0:T(8,128)(2,1)} %param.7) | copy-start | bytes 9437188
  7.2 62.2 %all-gather.2.cloned.1.call-start = ((), (), s32[]{:S(2)}) async-start(), calls=%async_computation.4 | async-start | bytes 2924544 | tf_op jit(solution)/shard_map/all_gather | solution.py:29
  10.2 178.2 %reduce-scatter.3.cloned.1.call-start = ((), (), s32[]{:S(2)}) async-start(), calls=%async_computation.5 | async-start | bytes 7798784 | tf_op jit(solution)/shard_map/reduce_scatter | solution.py:31
  89.2 0.7 copy-start.4
  92.4 98.7 %all-to-all-start = ((s32[16,1,28]{2,1,0:T(1,128)}), s32[16,1,28]{2,1,0:T(1,128)S(1)}, u32[]{:S(2)}, u32[]{:S(2)}) async-start(s32[16,1,28]{2,1,0:T(1,128)} %sub.18), calls=%async_computation.1 | async-start | bytes 16384 | tf_op jit(solution)/shard_map/all_to_all | solution.py:59
  189.4 33.1 %copy-start.2 = (bf16[112,1024]{1,0:T(8,128)(2,1)}, bf16[112,1024]{1,0:T(8,128)(2,1)S(1)}, u32[]{:S(2)}) copy-start(bf16[112,1024]{1,0:T(8,128)(2,1)S(1)} %convert_element_type.40) | copy-start | bytes 688132
  191.0 31.3 %all-to-all-start.1 = ((bf16[16,28,1024]{2,1,0:T(8,128)(2,1)}), bf16[16,28,1024]{2,1,0:T(8,128)(2,1)S(1)}, u32[]{:S(2)}, u32[]{:S(2)}) async-start(bf16[16,28,1024]{2,1,0:T(8,128)(2,1)} %reshape.105), calls=%async_computation.2 | async-start | bytes 2097152 | tf_op jit(solution)/shard_map/all_to_all | solution.py:58
  199.0 102.9 %reduce-scatter.5.cloned.1.call-start = ((), (), s32[]{:S(2)}) async-start(), calls=%async_computation.6 | async-start | bytes 2228224 | tf_op jit(solution)/shard_map/reduce_scatter | solution.py:68
  222.5 79.4 %copy-start.3 = (f32[1024,64]{0,1:T(8,128)S(1)}, f32[1024,64]{0,1:T(8,128)}, u32[]{:S(2)}) copy-start(f32[1024,64]{0,1:T(8,128)} %param.11) | copy-start | bytes 786436
Sparse Core Ops, SparseCore 0:
  11.3 58.0 all-gather.1
  89.3 99.0 reduce-scatter.2
  225.5 76.3 reduce-scatter.4
where the time goes:
time: 313 us; the launch traced here: 310 us
  waiting for transfers between devices  212 us (68%)
  blocking collectives  31.5 us (10%)
  matrix products  23 us (7%)
  starting transfers between devices  16.1 us (5%)
  between operations  13.9 us (4%)
  other arithmetic  9.7 us (3%)
  local copies, waits for them, and re-layouts  4.45 us (1%)
    reduce_scatter x1, waiting for transfers between devices, per_device(): lax.psum_scatter(jnp.dot(kernel_all, factor, preferred_element_type=jnp.f...  88.1 us
    all_gather x1, waiting for transfers between devices, per_device(): lax.all_gather(unit_points, 'land', axis=0, tiled=True)  56.6 us
    reduce_scatter x1, waiting for transfers between devices, per_device(): lax.psum_scatter(part_totals.astype(jnp.bfloat16), 'land', scatter_dimens...  44.8 us
    psum x1, blocking collectives, per_device(): counts = lax.psum(part_counts, 'land')  31.5 us
    all_to_all x1, waiting for transfers between devices, per_device(): lax.all_to_all(packed, 'dp', split_axis=0, concat_axis=0, tiled=True)  22 us
    dot_general x1, matrix products, per_device(): jnp.dot(kernel_all, factor, preferred_element_type=jnp.float32)  19.8 us
    all_to_all x1, starting transfers between devices, per_device(): lax.all_to_all(packed, 'dp', split_axis=0, concat_axis=0, tiled=True)  8.01 us
    all_to_all x1, starting transfers between devices, per_device(): lax.all_to_all(labels, 'dp', split_axis=0, concat_axis=0, tiled=True)  7.93 us
  transfers between devices with their start and end apart: 5, of which 4 were waited for; matrix products, arithmetic and copies ran while one was open for 3% of the time, Pallas kernels for 0%

commit v1 on v0

v1 whole, which is shorter than its diff:
```python
import functools
import math

import jax
import jax.numpy as jnp
from jax import lax
from jax.experimental import pallas as pl
from jax.experimental.pallas import tpu as pltpu
from jax.sharding import PartitionSpec as P

MESH = pl.DeviceIdType.MESH
F32 = jnp.float32
BF16 = jnp.bfloat16

EMB = 768
RANK = 1024
PTS = 112
SRC = 8
OWN = 16
KD = 1024
ROWS = (32, 32, 32, 16)
CAPS = (8, 8, 8, 4)
STARTS = (0, 32, 64, 96)
CHUNKS = 4
TILE = 1024
LM = 2048
COLS = 128
NT = (((1,), (1,)), ((), ()))


def unit_rows(values):
    widened = values.astype(F32)
    squared_sum = jnp.sum(widened * widened, axis=1, keepdims=True) + 1e-06
    return (widened * lax.rsqrt(squared_sum)).astype(BF16)


def body(
    sharpness,
    points_ref,
    perm_ref,
    back_ref,
    meta_ref,
    land_ref,
    factor_ref,
    old_ref,
    feat_ref,
    cent_ref,
    land,
    fac,
    metas,
    sorted_pts,
    featq,
    counts,
    pcounts,
    totals,
    flipped,
    ptotals,
    lab_send,
    lab_recv,
    ag,
    acc,
    ppart,
    rs_send,
    rs_recv,
    poh,
    oh,
    dp_send,
    dp_recv,
    local_sem,
    meta_sems,
    ag_sems,
    fwd_sems,
    pair_sems,
    rs_sems,
    back_sems,
    lab_sems,
    dp_sems,
    fin_sems,
):
    dp = lax.axis_index("dp")
    la = lax.axis_index("land")
    me = la // 2
    core = la % 2
    ylo = dp % 2
    z = dp // 2

    def chip(delta):
        other = (me + delta) % SRC
        lo = (ylo + me % 2 + other % 2) % 2
        return {"dp": z * 2 + lo, "land": other * 2 + core}

    def owner(delta):
        return {"dp": (dp + delta) % OWN, "land": la}

    partner = {"dp": dp, "land": me * 2 + 1 - core}

    def send(src, dst, sems, slot, device):
        return pltpu.make_async_remote_copy(
            src_ref=src,
            dst_ref=dst,
            send_sem=sems.at[(0,) + slot],
            recv_sem=sems.at[(1,) + slot],
            device_id=device,
            device_id_type=MESH,
        )

    def meta_copy(delta):
        return send(meta_ref, metas.at[delta], meta_sems, (delta,), chip(delta))

    def ag_copy(k, delta):
        n = ROWS[k]
        return send(
            sorted_pts.at[pl.ds(STARTS[k], n), :],
            ag[k].at[pl.ds(pl.multiple_of(me * n, n), n), :],
            ag_sems,
            (k, delta),
            chip(delta),
        )

    def fwd_copy(k):
        n = ROWS[k] * SRC
        return send(ag[k].at[pl.ds(0, n), :], ag[k].at[pl.ds(n, n), :], fwd_sems, (k,), partner)

    def pair_copy(k):
        n = ROWS[k] * SRC
        return send(acc[k].at[pl.ds(n, n), :], ppart[k], pair_sems, (k,), partner)

    def rs_copy(k, delta):
        return send(rs_send[k].at[delta], rs_recv[k].at[delta], rs_sems, (k, delta), chip(delta))

    def back_copy(k, delta):
        n = ROWS[k]
        other = (me + delta) % SRC
        return send(
            dp_recv_feat(k).at[pl.ds(pl.multiple_of(other * n, n), n), :],
            featq.at[pl.ds(STARTS[k], n), pl.ds(pl.multiple_of(me * COLS, COLS), COLS)],
            back_sems,
            (k, delta),
            chip(delta),
        )

    def dp_recv_feat(k):
        return rs_recv[k].at[0]

    def lab_copy(delta):
        return send(
            lab_send.at[(dp + delta) % OWN], lab_recv.at[dp], lab_sems, (delta,), owner(delta)
        )

    def dp_copy(k, delta):
        n = SRC * CAPS[k]
        to = (dp + delta) % OWN
        return send(
            dp_send[k].at[pl.ds(pl.multiple_of(to * n, n), n), :],
            dp_recv[k].at[pl.ds(pl.multiple_of(dp * n, n), n), :],
            dp_sems,
            (k, delta),
            owner(delta),
        )

    def count_copy():
        return send(counts, pcounts, fin_sems, (0,), partner)

    def total_copy():
        half = pl.ds(pl.multiple_of((1 - core) * 64, 64), 64)
        return send(flipped.at[half, :], ptotals, fin_sems, (1,), partner)

    barrier = pltpu.get_barrier_semaphore()
    pl.semaphore_signal(barrier, inc=1, device_id=partner, device_id_type=MESH)
    for delta in range(1, SRC):
        pl.semaphore_signal(barrier, inc=1, device_id=chip(delta), device_id_type=MESH)
    for delta in range(1, OWN):
        pl.semaphore_signal(barrier, inc=1, device_id=owner(delta), device_id_type=MESH)
    load_land = pltpu.make_async_copy(land_ref, land, local_sem.at[0])
    load_fac = pltpu.make_async_copy(factor_ref, fac, local_sem.at[1])
    load_land.start()
    load_fac.start()

    unit_points = unit_rows(points_ref[...])
    sorted_pts[...] = jnp.dot(perm_ref[...], unit_points, preferred_element_type=F32).astype(BF16)
    for k in range(CHUNKS):
        n = ROWS[k]
        ag[k][pl.ds(pl.multiple_of(me * n, n), n), :] = sorted_pts[STARTS[k] : STARTS[k] + n, :]

    pl.semaphore_wait(barrier, SRC + OWN - 1)

    for delta in range(1, SRC):
        ag_copy(0, delta).start()
    for delta in range(1, SRC):
        meta_copy(delta).start()
    for k in range(1, CHUNKS):
        for delta in range(1, SRC):
            ag_copy(k, delta).start()

    load_land.wait()

    @pl.loop(0, LM // 256)
    def _(t):
        rows = pl.ds(pl.multiple_of(t * 256, 256), 256)
        land[rows, :] = unit_rows(land[rows, :])

    load_fac.wait()

    def gather_chunk(k):
        for delta in range(1, SRC):
            ag_copy(k, delta).wait_recv()
        fwd_copy(k).start()

    scale = sharpness * math.log2(math.e)

    def matmul(k, part):
        n = ROWS[k] * SRC
        mine = pl.ds(part * n, n)
        for t in range(LM // TILE):
            rows = pl.ds(t * TILE, TILE)
            scores = lax.dot_general(ag[k][mine, :], land[rows, :], NT, preferred_element_type=F32)
            kernel = jnp.exp2(scores * scale).astype(BF16)
            share = jnp.dot(kernel, fac[rows, :], preferred_element_type=F32)
            if t == 0:
                acc[k][mine, :] = share
            else:
                acc[k][mine, :] += share

    def labels():
        for delta in range(1, SRC):
            meta_copy(delta).wait_recv()
        merged = meta_ref[...]
        for delta in range(1, SRC):
            merged = merged + metas[delta]
        owners_col = lax.broadcasted_iota(jnp.int32, (OWN, 256), 0)
        lane_col = lax.broadcasted_iota(jnp.int32, (COLS, 256), 0)
        found = []
        for k in range(CHUNKS):
            n = SRC * CAPS[k]
            pts = ROWS[k] * SRC
            code = merged[k : k + 1, :pts] - 1
            local = merged[CHUNKS + k : CHUNKS + k + 1, :pts]
            slot = lax.broadcasted_iota(jnp.int32, (OWN * n, pts), 0)
            poh[k][...] = jnp.where(slot == code, 1.0, 0.0).astype(BF16)
            to = code // n
            lane = code - to * n + (dp % (COLS // n)) * n
            hit = owners_col[:, :pts] == to
            high = jnp.where(hit, local // 32, 0).astype(F32).astype(BF16)
            low = jnp.where(hit, local % 32, 0).astype(F32).astype(BF16)
            place = jnp.where(lane_col[:, :pts] == lane, 1.0, 0.0).astype(BF16)
            high = lax.dot_general(high, place, NT, preferred_element_type=F32)
            low = lax.dot_general(low, place, NT, preferred_element_type=F32)
            found.append((high * 32.0 + low).astype(jnp.int32))
        for o in range(OWN):
            for k in range(CHUNKS):
                lab_send[o, :, k * COLS : (k + 1) * COLS] = found[k][o : o + 1, :]
        for delta in range(1, OWN):
            lab_copy(delta).start()
        lab_recv[dp] = lab_send[dp]

    def hits():
        for delta in range(1, OWN):
            lab_copy(delta).wait_recv()
        cluster = lax.broadcasted_iota(jnp.int32, (KD, COLS), 0) + 1
        for k in range(CHUNKS):
            share = COLS // (SRC * CAPS[k])
            for m in range(OWN // share):
                label = lab_recv[m * share][:, k * COLS : (k + 1) * COLS]
                for i in range(1, share):
                    label = label + lab_recv[m * share + i][:, k * COLS : (k + 1) * COLS]
                hit = jnp.where(cluster == label, 1.0, 0.0).astype(BF16)
                oh[k][:, m * COLS : (m + 1) * COLS] = hit
        ones = jnp.ones((OWN * SRC * CAPS[0], COLS), BF16)
        total = jnp.dot(oh[0][...], ones, preferred_element_type=F32)
        for k in range(1, CHUNKS):
            total += jnp.dot(oh[k][...], ones[: OWN * SRC * CAPS[k]], preferred_element_type=F32)
        counts[...] = total
        count_copy().start()

    def scatter(k):
        n = ROWS[k] * SRC
        pair_copy(k).wait_recv()
        for delta in range(1, SRC):
            other = pl.ds(pl.multiple_of((me + delta) % SRC * COLS, COLS), COLS)
            both = acc[k][pl.ds(0, n), other] + ppart[k][:, other]
            rs_send[k][delta] = both.astype(BF16)
            rs_copy(k, delta).start()

    def reduce_rows(k):
        n = ROWS[k]
        here = pl.ds(pl.multiple_of(me * COLS, COLS), COLS)
        rows = acc[k][pl.ds(0, n * SRC), here] + ppart[k][:, here]
        for delta in range(1, SRC):
            rs_copy(k, delta).wait_recv()
            rows = rows + rs_recv[k][delta].astype(F32)
        rows = rows.astype(BF16)
        packed = jnp.dot(poh[k][...], rows, preferred_element_type=F32)
        dp_send[k][...] = packed.astype(BF16)
        for delta in range(1, OWN):
            dp_copy(k, delta).start()
        m = SRC * CAPS[k]
        mine = pl.ds(pl.multiple_of(dp * m, m), m)
        dp_recv[k][mine, :] = dp_send[k][mine, :]
        rs_recv[k][0] = rows
        for delta in range(1, SRC):
            back_copy(k, delta).start()
        featq[STARTS[k] : STARTS[k] + n, here] = rs_recv[k][
            0, pl.ds(pl.multiple_of(me * n, n), n), :
        ]

    def add_owned(k):
        for delta in range(1, OWN):
            dp_copy(k, delta).wait_recv()
        total = jnp.dot(oh[k][...], dp_recv[k][...], preferred_element_type=F32)
        if k == 0:
            totals[...] = total
        else:
            totals[...] += total

    gather_chunk(0)
    matmul(0, 0)
    fwd_copy(0).wait_recv()
    gather_chunk(1)
    matmul(0, 1)
    pair_copy(0).start()
    labels()
    for k in range(1, CHUNKS):
        fwd_copy(k).wait_recv()
        matmul(k, 1)
        pair_copy(k).start()
        scatter(k - 1)
        if k + 1 < CHUNKS:
            gather_chunk(k + 1)
        matmul(k, 0)
        if k == 1:
            hits()
        if k >= 2:
            reduce_rows(k - 2)
        if k >= 3:
            add_owned(k - 3)
    scatter(CHUNKS - 1)
    reduce_rows(CHUNKS - 2)
    add_owned(CHUNKS - 3)
    reduce_rows(CHUNKS - 1)
    add_owned(CHUNKS - 2)
    for k in range(CHUNKS):
        for delta in range(1, SRC):
            back_copy(k, delta).wait_recv()
    feat_ref[...] = jnp.dot(back_ref[...], featq[...], preferred_element_type=F32).astype(BF16)
    count_copy().wait_recv()
    add_owned(CHUNKS - 1)

    flipped[...] = totals[...].T
    total_copy().start()
    seen = (counts[...] + pcounts[...]).T[:64]
    safe = jnp.maximum(seen, 1.0)
    old = old_ref[...]
    total_copy().wait_recv()
    mine = flipped[pl.ds(pl.multiple_of(core * 64, 64), 64), :] + ptotals[...]
    cent_ref[...] = jnp.where(seen > 0, mine / safe, old)

    for delta in range(1, SRC):
        meta_copy(delta).wait_send()
    for delta in range(1, OWN):
        lab_copy(delta).wait_send()
    for k in range(CHUNKS):
        fwd_copy(k).wait_send()
        pair_copy(k).wait_send()
        for delta in range(1, SRC):
            ag_copy(k, delta).wait_send()
            rs_copy(k, delta).wait_send()
            back_copy(k, delta).wait_send()
        for delta in range(1, OWN):
            dp_copy(k, delta).wait_send()
    count_copy().wait_send()
    total_copy().wait_send()


def per_device(points, landmarks, factor, assignments, owner_map, old_centroids):
    sharpness = math.sqrt(points.shape[1])
    chip = lax.axis_index("land") // 2
    slot_ids = jnp.take(owner_map, assignments)
    owner_ids = slot_ids // KD
    local_ids = slot_ids % KD
    hits = (owner_ids[:, None] == jnp.arange(OWN, dtype=jnp.int32)[None, :]).astype(jnp.int32)
    before = jnp.cumsum(hits, axis=0) - hits
    rank = jnp.sum(before * hits, axis=1)
    smaller = jnp.sum((owner_ids[None, :] < owner_ids[:, None]).astype(jnp.int32), axis=1)
    place = smaller + rank
    part = place % 7
    index = part * 16 + place // 7
    turn = rank // 7
    chunk = part // 2
    last = chunk == 3
    step = jnp.where(last, turn, (part % 2) * 4 + turn)
    cap = jnp.where(last, 4, 8)
    code = owner_ids * (SRC * cap) + chip * cap + step
    lane = chip * jnp.where(last, 16, 32) + index - chunk * 32
    perm = jnp.arange(PTS, dtype=jnp.int32)[:, None] == index[None, :]
    back = index[:, None] == jnp.arange(PTS, dtype=jnp.int32)[None, :]
    rows = jnp.arange(8, dtype=jnp.int32)[:, None, None]
    lanes = jnp.arange(256, dtype=jnp.int32)[None, :, None]
    values = jnp.where(rows < 4, code + 1, local_ids + 1)
    meta = jnp.sum(jnp.where((rows % 4 == chunk) & (lanes == lane), values, 0), axis=2)

    vmem = pl.BlockSpec(memory_space=pltpu.VMEM)
    hbm = pl.BlockSpec(memory_space=pl.ANY)
    chunks = range(CHUNKS)
    features, centroids = pl.pallas_call(
        functools.partial(body, sharpness),
        out_shape=(
            jax.ShapeDtypeStruct((PTS, RANK), BF16),
            jax.ShapeDtypeStruct((64, KD), F32),
        ),
        in_specs=[vmem, vmem, vmem, vmem, hbm, hbm, vmem],
        out_specs=(vmem, vmem),
        scratch_shapes=[
            pltpu.VMEM((LM, EMB), BF16),
            pltpu.VMEM((LM, RANK), BF16),
            pltpu.VMEM((SRC, 8, 256), jnp.int32),
            pltpu.VMEM((PTS, EMB), BF16),
            pltpu.VMEM((PTS, RANK), BF16),
            pltpu.VMEM((KD, COLS), F32),
            pltpu.VMEM((KD, COLS), F32),
            pltpu.VMEM((KD, COLS), F32),
            pltpu.VMEM((COLS, KD), F32),
            pltpu.VMEM((64, KD), F32),
            pltpu.VMEM((OWN, 1, CHUNKS * COLS), jnp.int32),
            pltpu.VMEM((OWN, 1, CHUNKS * COLS), jnp.int32),
            [pltpu.VMEM((2 * SRC * ROWS[k], EMB), BF16) for k in chunks],
            [pltpu.VMEM((2 * SRC * ROWS[k], RANK), F32) for k in chunks],
            [pltpu.VMEM((SRC * ROWS[k], RANK), F32) for k in chunks],
            [pltpu.VMEM((SRC, SRC * ROWS[k], COLS), BF16) for k in chunks],
            [pltpu.VMEM((SRC, SRC * ROWS[k], COLS), BF16) for k in chunks],
            [pltpu.VMEM((OWN * SRC * CAPS[k], SRC * ROWS[k]), BF16) for k in chunks],
            [pltpu.VMEM((KD, OWN * SRC * CAPS[k]), BF16) for k in chunks],
            [pltpu.VMEM((OWN * SRC * CAPS[k], COLS), BF16) for k in chunks],
            [pltpu.VMEM((OWN * SRC * CAPS[k], COLS), BF16) for k in chunks],
            pltpu.SemaphoreType.DMA((2,)),
            pltpu.SemaphoreType.DMA((2, SRC)),
            pltpu.SemaphoreType.DMA((2, CHUNKS, SRC)),
            pltpu.SemaphoreType.DMA((2, CHUNKS)),
            pltpu.SemaphoreType.DMA((2, CHUNKS)),
            pltpu.SemaphoreType.DMA((2, CHUNKS, SRC)),
            pltpu.SemaphoreType.DMA((2, CHUNKS, SRC)),
            pltpu.SemaphoreType.DMA((2, OWN)),
            pltpu.SemaphoreType.DMA((2, CHUNKS, OWN)),
            pltpu.SemaphoreType.DMA((2, 2)),
        ],
        name="nystrom",
        compiler_params=pltpu.CompilerParams(
            collective_id=1, has_side_effects=True, vmem_limit_bytes=60 * 2**20
        ),
    )(
        points,
        perm.astype(BF16),
        back.astype(BF16),
        meta,
        landmarks,
        factor,
        old_centroids.T,
    )
    return (features, centroids.T)


def solution(mesh):
    in_specs = (
        P(("dp", "land"), None),
        P("land", None),
        P("land", None),
        P(("dp", "land")),
        P(),
        P("dp", "land"),
    )
    out_specs = (P(("dp", "land"), None), P("dp", "land"))
    return jax.shard_map(
        per_device, mesh=mesh, in_specs=in_specs, out_specs=out_specs, check_vma=False
    )
```

time: 313 us -> 84.4 us (0.27)
  waiting for transfers between devices: 212 us -> 0 us
  Pallas kernels: 0 us -> 74.4 us
  blocking collectives: 31.5 us -> 0 us
  matrix products: 23 us -> 0 us
  starting transfers between devices: 16.1 us -> 0 us
  between operations: 13.9 us -> 0.72 us
  other arithmetic: 9.7 us -> 4.51 us
    reduce_scatter x2 -> x0, waiting for transfers between devices: 133 us -> none  [the longest x1 88.1 us: per_device(): lax.psum_scatter(jnp.dot(kernel_all, factor, preferred_element_type=jnp.f...]
    pallas_call x0 -> x1, Pallas kernels: none -> 74.4 us  [per_device(): pl.pallas_call(functools.partial(body, sharpness), out_shape=(jax.ShapeDt...]
    all_gather x1 -> x0, waiting for transfers between devices: 56.6 us -> none  [per_device(): lax.all_gather(unit_points, 'land', axis=0, tiled=True)]
    psum x1 -> x0, blocking collectives: 31.5 us -> none  [per_device(): counts = lax.psum(part_counts, 'land')]
    dot_general x3 -> x0, matrix products: 23 us -> none  [the longest x1 19.8 us: per_device(): jnp.dot(kernel_all, factor, preferred_element_type=jnp.float32)]
    all_to_all x2 -> x0, waiting for transfers between devices: 22 us -> none  [the longest x1 22 us: per_device(): lax.all_to_all(packed, 'dp', split_axis=0, concat_axis=0, tiled=True)]
    all_to_all x2 -> x0, starting transfers between devices: 15.9 us -> none  [the longest x1 8.01 us: per_device(): lax.all_to_all(packed, 'dp', split_axis=0, concat_axis=0, tiled=True)]
  transfers between devices with their start and end apart: 5 -> 0, of which waited for: 4 -> 0; matrix products, arithmetic and copies ran while one was open for 3% -> 0% of each run, Pallas kernels for 0% -> 0%
where the time goes in v1:
time: 84.4 us; the launch traced here: 84.2 us
  Pallas kernels  74.4 us (88%)
  local copies, waits for them, and re-layouts  4.57 us (5%)
  other arithmetic  4.51 us (5%)
    pallas_call x1, Pallas kernels, per_device(): pl.pallas_call(functools.partial(body, sharpness), out_shape=(jax.ShapeDt...  74.4 us
    unnamed x4, local copies, waits for them, and re-layouts  3.42 us

profile of v1, /device:TPU:11, one launch (start us, length us, event | category | flops | bytes accessed | tf_op | source)
XLA Modules:
  0.0 84.2 jit_solution(6823864031079120257)
XLA Ops:
  0.6 0.0 copy-start
  0.7 0.7 compare_select_fusion
  1.4 0.1 copy-done
  1.5 1.1 %gather_fusion = s32[112]{0:T(128)S(1)} fusion(s32[16384]{0:T(1024)S(1)} %copy-done, s32[1024]{0:T(1024)S(1)} %pad_clamp_fusion), kind=kCustom, calls=%fused_computation | custom fusion | bytes 1344 | tf_op jit(solution)/shard_map/jit(_take)/gather | solution.py:377
  2.6 0.7 fusion.5
  3.3 0.7 and_select_fusion.7
  4.0 0.2 convert_reduce_fusion
  4.1 0.1 fusion
  4.2 0.2 reduce_window_sum.11
  4.4 0.2 select_reduce_fusion.1
  4.6 0.1 broadcast_compare_fusion
  4.7 0.1 broadcast_select_fusion
  4.8 0.1 iota_compare_fusion
  4.9 0.9 %select_reduce_fusion.meta_ref = s32[8,256]{1,0:T(8,128)} fusion(s32[8,112]{1,0:T(8,128)S(1)} %broadcast_select_fusion, pred[256,112]{0,1:T(8,128)(4,1)S(1)} %iota_compare_fusion, pred[8,112]{1,0:T(8,128)(4,1)S(1)} %broadcast_compare_fusion), kind=kLoop, calls=%fused_computation.1 | loop fusion | flops 686080 | bytes 41344 | tf_op jit(solution)/shard_map/reduce_sum | solution.py:399
  5.8 0.7 fusion.2
  6.5 74.4 %nystrom.1 = (bf16[112,1024]{1,0:T(8,128)(2,1)}, f32[64,1024]{1,0:T(8,128)}) custom-call(bf16[112,768]{1,0:T(8,128)(2,1)} %points_ref.1, bf16[112,112]{1,0:T(8,128)(2,1)} %get-tuple-element.13.perm_ref, bf16[112,112]{1,0:T(8,128)(2,1)} %get-tuple-element.12.back_ref, s32[8,256]{1,0:T(8,128)} %select_reduce_fusion.meta_ref, bf16[2048,768]{1,0:T(8,128)(2,1)} %land_ref.1, ...), custom_call_target="tpu_custom_call" | custom-call | tf_op jit(solution)/shard_map/nystrom/pallas_call | solution.py:404
  80.9 1.6 %copy.10 = bf16[112,1024]{1,0:T(8,128)(2,1)} copy(bf16[112,1024]{1,0:T(8,128)(2,1)} %get-tuple-element.16) | data formatting | bytes 458752
  82.5 1.7 %copy.11 = f32[1024,64]{0,1:T(8,128)} copy(f32[1024,64]{0,1:T(8,128)} %bitcast.3) | data formatting | bytes 524288
  (5 shorter events, 0.1 us)
Async XLA Ops:
  0.6 0.8 %copy-start = (s32[16384]{0:T(1024)S(1)}, s32[16384]{0:T(1024)}, u32[]{:S(2)}) copy-start(s32[16384]{0:T(1024)} %param.10) | copy-start | bytes 196612

commit v2 on v1

v2 whole, which is shorter than its diff:
```python
import functools
import math

import jax
import jax.numpy as jnp
from jax import lax
from jax.experimental import pallas as pl
from jax.experimental.pallas import tpu as pltpu
from jax.sharding import PartitionSpec as P

MESH = pl.DeviceIdType.MESH
F32 = jnp.float32
BF16 = jnp.bfloat16

EMB = 768
RANK = 1024
PTS = 112
SRC = 8
OWN = 16
KD = 1024
ROWS = (32, 32, 32, 16)
CAPS = (8, 8, 8, 4)
STARTS = (0, 32, 64, 96)
CHUNKS = 4
TILE = 1024
LM = 2048
COLS = 128
NT = (((1,), (1,)), ((), ()))


def unit_rows(values):
    widened = values.astype(F32)
    squared_sum = jnp.sum(widened * widened, axis=1, keepdims=True) + 1e-06
    return (widened * lax.rsqrt(squared_sum)).astype(BF16)


def body(
    sharpness,
    points_ref,
    assign_ref,
    table_ref,
    land_ref,
    factor_ref,
    featq,
    back_ref,
    sums_ref,
    seen_ref,
    land,
    fac,
    meta,
    metas,
    sorted_pts,
    counts,
    pcounts,
    totals,
    flipped,
    ptotals,
    lab_send,
    lab_recv,
    ag,
    acc,
    ppart,
    rs_send,
    rs_recv,
    poh,
    oh,
    dp_send,
    dp_recv,
    local_sem,
    meta_sems,
    ag_sems,
    fwd_sems,
    pair_sems,
    rs_sems,
    back_sems,
    lab_sems,
    dp_sems,
    fin_sems,
):
    dp = lax.axis_index("dp")
    la = lax.axis_index("land")
    me = la // 2
    core = la % 2
    ylo = dp % 2
    z = dp // 2

    def mirror(chip):
        return chip + 1 - 2 * (chip % 2)

    right = (me + 2) % SRC
    left = (me + 6) % SRC
    far = (me + 4) % SRC
    near = mirror(me)

    def device(chip):
        lo = (ylo + me % 2 + chip % 2) % 2
        return {"dp": z * 2 + lo, "land": chip * 2 + core}

    def owner(delta):
        return {"dp": (dp + delta) % OWN, "land": la}

    partner = {"dp": dp, "land": me * 2 + 1 - core}

    def send(src, dst, sems, slot, to):
        return pltpu.make_async_remote_copy(
            src_ref=src,
            dst_ref=dst,
            send_sem=sems.at[(0,) + slot],
            recv_sem=sems.at[(1,) + slot],
            device_id=to,
            device_id_type=MESH,
        )

    def at(index, size):
        return pl.ds(pl.multiple_of(index * size, size), size)

    def meta_copy(delta):
        return send(meta, metas.at[delta], meta_sems, (delta,), device((me + delta) % SRC))

    ag_steps = ((me, near), (me, right), (me, left), (me, far), (near, right), (near, left), (far, near))

    def ag_copy(k, step):
        block, to = ag_steps[step]
        n = ROWS[k]
        src = sorted_pts.at[pl.ds(STARTS[k], n), :] if step < 4 else ag[k].at[at(block, n), :]
        return send(src, ag[k].at[at(block, n), :], ag_sems, (k, step), device(to))

    def fwd_copy(k):
        n = ROWS[k] * SRC
        return send(ag[k].at[pl.ds(0, n), :], ag[k].at[pl.ds(n, n), :], fwd_sems, (k,), partner)

    def pair_copy(k):
        n = ROWS[k] * SRC
        return send(acc[k].at[pl.ds(n, n), :], ppart[k], pair_sems, (k,), partner)

    rs_steps = (
        (right, mirror(right)),
        (left, mirror(left)),
        (near, mirror(far)),
        (right, right),
        (left, left),
        (far, far),
        (near, near),
    )

    def rs_copy(k, step):
        if k == CHUNKS - 1:
            to = (me + step + 1) % SRC
        else:
            to = rs_steps[step][0]
        return send(rs_send[k].at[step], rs_recv[k].at[step], rs_sems, (k, step), device(to))

    def back_copy(k, delta):
        other = (me + delta) % SRC
        return send(
            rs_recv[k].at[7].at[at(other, ROWS[k]), :],
            featq.at[pl.ds(STARTS[k], ROWS[k]), at(me, COLS)],
            back_sems,
            (k, delta),
            device(other),
        )

    def lab_copy(delta):
        return send(
            lab_send.at[(dp + delta) % OWN], lab_recv.at[dp], lab_sems, (delta,), owner(delta)
        )

    def dp_copy(k, delta):
        n = SRC * CAPS[k]
        return send(
            dp_send[k].at[at((dp + delta) % OWN, n), :],
            dp_recv[k].at[at(dp, n), :],
            dp_sems,
            (k, delta),
            owner(delta),
        )

    def count_copy():
        return send(counts, pcounts, fin_sems, (0,), partner)

    def total_copy():
        return send(flipped.at[at(1 - core, 64), :], ptotals, fin_sems, (1,), partner)

    barrier = pltpu.get_barrier_semaphore()
    pl.semaphore_signal(barrier, inc=1, device_id=partner, device_id_type=MESH)
    for delta in range(1, SRC):
        pl.semaphore_signal(
            barrier, inc=1, device_id=device((me + delta) % SRC), device_id_type=MESH
        )
    for delta in range(1, OWN):
        pl.semaphore_signal(barrier, inc=1, device_id=owner(delta), device_id_type=MESH)
    load_land = pltpu.make_async_copy(land_ref, land, local_sem.at[0])
    load_fac = pltpu.make_async_copy(factor_ref, fac, local_sem.at[1])
    load_land.start()
    load_fac.start()

    def iota(rows, lanes):
        return lax.broadcasted_iota(jnp.int32, (rows, lanes), 0)

    def one_hot(cond):
        return jnp.where(cond, 1.0, 0.0).astype(BF16)

    def small(values):
        return values.astype(F32).astype(BF16)

    assign = assign_ref[...]
    table = table_ref[...]
    picked = one_hot(iota(128, PTS) == assign // 128)
    lane_hit = iota(128, PTS) == assign % 128

    def look_up(values):
        rows = jnp.dot(small(values.T), picked, preferred_element_type=F32)
        return jnp.sum(jnp.where(lane_hit, rows, 0.0), axis=0, keepdims=True).astype(jnp.int32)

    owner_ids = look_up(table // KD)
    high_ids = look_up(table % KD // 32)
    low_ids = look_up(table % 32)
    hits_of = iota(OWN, PTS) == owner_ids
    earlier = one_hot(iota(PTS, PTS) < lax.broadcasted_iota(jnp.int32, (PTS, PTS), 1))
    before = jnp.dot(one_hot(hits_of), earlier, preferred_element_type=F32)
    rank = jnp.sum(jnp.where(hits_of, before, 0.0), axis=0, keepdims=True).astype(jnp.int32)
    sizes = jnp.sum(jnp.where(hits_of, 1.0, 0.0), axis=1, keepdims=True)
    smaller = jnp.sum(
        jnp.where(iota(OWN, PTS) < owner_ids, sizes, 0.0), axis=0, keepdims=True
    ).astype(jnp.int32)
    place = smaller + rank
    part = place % 7
    index = part * 16 + place // 7
    perm = one_hot(iota(PTS, PTS) == index)
    sorted_pts[...] = jnp.dot(
        perm, unit_rows(points_ref[...]), preferred_element_type=F32
    ).astype(BF16)
    back_ref[...] = perm
    turn = rank // 7
    chunk = part // 2
    last = chunk == CHUNKS - 1
    step = jnp.where(last, turn, part % 2 * 4 + turn)
    cap = jnp.where(last, CAPS[3], CAPS[0])
    code = owner_ids * (SRC * cap) + me * cap + step + 1
    lane = me * jnp.where(last, ROWS[3], ROWS[0]) + index - chunk * 32
    placed = one_hot(iota(256, PTS) == lane)
    mine = iota(CHUNKS, PTS) == chunk

    def spread(values):
        return lax.dot_general(
            small(jnp.where(mine, values, 0)), placed, NT, preferred_element_type=F32
        )

    labels_of = high_ids * 32 + low_ids + 1
    meta[0:4, :] = (spread(code // 32) * 32.0 + spread(code % 32)).astype(jnp.int32)
    meta[4:8, :] = (spread(labels_of // 32) * 32.0 + spread(labels_of % 32)).astype(jnp.int32)
    for k in range(CHUNKS):
        ag[k][at(me, ROWS[k]), :] = sorted_pts[STARTS[k] : STARTS[k] + ROWS[k], :]

    pl.semaphore_wait(barrier, SRC + OWN - 1)

    def ag_own(k):
        for i in range(4):
            ag_copy(k, i).start()

    def ag_forward(k):
        ag_copy(k, 0).wait_recv()
        ag_copy(k, 4).start()
        ag_copy(k, 5).start()
        ag_copy(k, 3).wait_recv()
        ag_copy(k, 6).start()
        if k + 2 < CHUNKS:
            ag_own(k + 2)

    def gather(k):
        for i in (1, 2, 4, 5, 6):
            ag_copy(k, i).wait_recv()
        fwd_copy(k).start()

    def normalize(first, last):
        @pl.loop(first, last)
        def _(t):
            rows = at(t, 256)
            land[rows, :] = unit_rows(land[rows, :])

    scale = sharpness * math.log2(math.e)

    def matmul(k, part):
        n = ROWS[k] * SRC
        mine = pl.ds(part * n, n) if part < 2 else pl.ds(0, 2 * n)
        for t in range(LM // TILE):
            rows = pl.ds(t * TILE, TILE)
            scores = lax.dot_general(ag[k][mine, :], land[rows, :], NT, preferred_element_type=F32)
            kernel = jnp.exp2(scores * scale).astype(BF16)
            share = jnp.dot(kernel, fac[rows, :], preferred_element_type=F32)
            if t == 0:
                acc[k][mine, :] = share
            else:
                acc[k][mine, :] += share

    def labels():
        for delta in range(1, SRC):
            meta_copy(delta).wait_recv()
        merged = meta[...]
        for delta in range(1, SRC):
            merged = merged + metas[delta]
        found = []
        for k in range(CHUNKS):
            n = SRC * CAPS[k]
            pts = ROWS[k] * SRC
            code = merged[k : k + 1, :pts] - 1
            local = merged[CHUNKS + k : CHUNKS + k + 1, :pts]
            poh[k][...] = one_hot(iota(OWN * n, pts) == code)
            to = code // n
            lane = code - to * n + (dp % (COLS // n)) * n
            hit = iota(OWN, pts) == to
            place = one_hot(iota(COLS, pts) == lane)
            high = small(jnp.where(hit, local // 32, 0))
            low = small(jnp.where(hit, local % 32, 0))
            high = lax.dot_general(high, place, NT, preferred_element_type=F32)
            low = lax.dot_general(low, place, NT, preferred_element_type=F32)
            found.append((high * 32.0 + low).astype(jnp.int32))
        for o in range(OWN):
            for k in range(CHUNKS):
                lab_send[o, :, k * COLS : (k + 1) * COLS] = found[k][o : o + 1, :]
        for delta in range(1, OWN):
            lab_copy(delta).start()
        lab_recv[dp] = lab_send[dp]

    def labels_arrived():
        for delta in range(1, OWN):
            lab_copy(delta).wait_recv()

    def hits(k):
        cluster = iota(KD, COLS) + 1
        share = COLS // (SRC * CAPS[k])
        for m in range(OWN // share):
            label = lab_recv[m * share][:, k * COLS : (k + 1) * COLS]
            for i in range(1, share):
                label = label + lab_recv[m * share + i][:, k * COLS : (k + 1) * COLS]
            oh[k][:, m * COLS : (m + 1) * COLS] = one_hot(cluster == label)
        ones = jnp.ones((OWN * SRC * CAPS[k], COLS), BF16)
        total = jnp.dot(oh[k][...], ones, preferred_element_type=F32)
        if k == 0:
            counts[...] = total
        else:
            counts[...] += total
        if k == CHUNKS - 1:
            count_copy().start()

    def both(k, chip):
        n = ROWS[k] * SRC
        cols = at(chip, COLS)
        return acc[k][pl.ds(0, n), cols] + ppart[k][:, cols]

    def scatter(k):
        pair_copy(k).wait_recv()
        for i in range(5):
            rs_send[k][i] = both(k, rs_steps[i][1]).astype(BF16)
            rs_copy(k, i).start()

    def scatter_sums(k):
        rs_copy(k, 2).wait_recv()
        rs_send[k][5] = (both(k, far) + rs_recv[k][2].astype(F32)).astype(BF16)
        rs_copy(k, 5).start()
        rs_copy(k, 0).wait_recv()
        rs_copy(k, 1).wait_recv()
        joined = both(k, near) + rs_recv[k][0].astype(F32) + rs_recv[k][1].astype(F32)
        rs_send[k][6] = joined.astype(BF16)
        rs_copy(k, 6).start()

    def scatter_last(k):
        pair_copy(k).wait_recv()
        for i in range(SRC - 1):
            rs_send[k][i] = both(k, (me + i + 1) % SRC).astype(BF16)
            rs_copy(k, i).start()

    def reduce_rows(k):
        n = ROWS[k]
        rows = both(k, me)
        for i in range(0 if k == CHUNKS - 1 else 3, 7):
            rs_copy(k, i).wait_recv()
            rows = rows + rs_recv[k][i].astype(F32)
        rows = rows.astype(BF16)
        packed = jnp.dot(poh[k][...], rows, preferred_element_type=F32)
        dp_send[k][...] = packed.astype(BF16)
        for delta in range(1, OWN):
            dp_copy(k, delta).start()
        m = SRC * CAPS[k]
        dp_recv[k][at(dp, m), :] = dp_send[k][at(dp, m), :]
        rs_recv[k][7] = rows
        for delta in range(1, SRC):
            back_copy(k, delta).start()
        featq[STARTS[k] : STARTS[k] + n, at(me, COLS)] = rs_recv[k][7, at(me, n), :]

    def add_owned(k):
        for delta in range(1, OWN):
            dp_copy(k, delta).wait_recv()
        total = jnp.dot(oh[k][...], dp_recv[k][...], preferred_element_type=F32)
        if k == 0:
            totals[...] = total
        else:
            totals[...] += total

    for delta in range(1, SRC):
        meta_copy(delta).start()
    ag_own(0)
    ag_own(1)
    load_land.wait()
    normalize(0, 4)
    ag_forward(0)
    normalize(4, 8)
    labels()
    load_fac.wait()
    gather(0)
    matmul(0, 0)
    ag_forward(1)
    fwd_copy(0).wait_recv()
    matmul(0, 1)
    pair_copy(0).start()
    gather(1)
    ag_forward(2)
    labels_arrived()
    hits(0)

    fwd_copy(1).wait_recv()
    matmul(1, 1)
    pair_copy(1).start()
    scatter(0)
    ag_forward(3)
    gather(2)
    matmul(1, 0)
    scatter_sums(0)

    fwd_copy(2).wait_recv()
    matmul(2, 1)
    pair_copy(2).start()
    scatter(1)
    gather(3)
    matmul(2, 0)
    scatter_sums(1)
    reduce_rows(0)

    fwd_copy(3).wait_recv()
    matmul(3, 2)
    pair_copy(3).start()
    scatter(2)
    hits(1)
    scatter_last(3)
    scatter_sums(2)
    hits(2)
    reduce_rows(1)
    hits(3)
    add_owned(0)
    reduce_rows(2)
    reduce_rows(3)
    add_owned(1)
    add_owned(2)
    for k in range(CHUNKS):
        for delta in range(1, SRC):
            back_copy(k, delta).wait_recv()
    count_copy().wait_recv()
    seen_ref[...] = (counts[...] + pcounts[...]).T[:8]
    add_owned(3)

    flipped[...] = totals[...].T
    total_copy().start()
    total_copy().wait_recv()
    sums_ref[...] = flipped[at(core, 64), :] + ptotals[...]

    for delta in range(1, SRC):
        meta_copy(delta).wait_send()
    for delta in range(1, OWN):
        lab_copy(delta).wait_send()
    for k in range(CHUNKS):
        fwd_copy(k).wait_send()
        pair_copy(k).wait_send()
        for i in range(7):
            ag_copy(k, i).wait_send()
            rs_copy(k, i).wait_send()
        for delta in range(1, SRC):
            back_copy(k, delta).wait_send()
        for delta in range(1, OWN):
            dp_copy(k, delta).wait_send()
    count_copy().wait_send()
    total_copy().wait_send()


def per_device(points, landmarks, factor, assignments, owner_map, old_centroids):
    sharpness = math.sqrt(points.shape[1])
    vmem = pl.BlockSpec(memory_space=pltpu.VMEM)
    hbm = pl.BlockSpec(memory_space=pl.ANY)
    chunks = range(CHUNKS)
    sorted_features, perm, sums, seen = pl.pallas_call(
        functools.partial(body, sharpness),
        out_shape=(
            jax.ShapeDtypeStruct((PTS, RANK), BF16),
            jax.ShapeDtypeStruct((PTS, PTS), BF16),
            jax.ShapeDtypeStruct((64, KD), F32),
            jax.ShapeDtypeStruct((8, KD), F32),
        ),
        in_specs=[vmem, vmem, vmem, hbm, hbm],
        out_specs=(vmem, vmem, vmem, vmem),
        scratch_shapes=[
            pltpu.VMEM((LM, EMB), BF16),
            pltpu.VMEM((LM, RANK), BF16),
            pltpu.VMEM((8, 256), jnp.int32),
            pltpu.VMEM((SRC, 8, 256), jnp.int32),
            pltpu.VMEM((PTS, EMB), BF16),
            pltpu.VMEM((KD, COLS), F32),
            pltpu.VMEM((KD, COLS), F32),
            pltpu.VMEM((KD, COLS), F32),
            pltpu.VMEM((COLS, KD), F32),
            pltpu.VMEM((64, KD), F32),
            pltpu.VMEM((OWN, 1, CHUNKS * COLS), jnp.int32),
            pltpu.VMEM((OWN, 1, CHUNKS * COLS), jnp.int32),
            [pltpu.VMEM((2 * SRC * ROWS[k], EMB), BF16) for k in chunks],
            [pltpu.VMEM((2 * SRC * ROWS[k], RANK), F32) for k in chunks],
            [pltpu.VMEM((SRC * ROWS[k], RANK), F32) for k in chunks],
            [pltpu.VMEM((SRC, SRC * ROWS[k], COLS), BF16) for k in chunks],
            [pltpu.VMEM((SRC, SRC * ROWS[k], COLS), BF16) for k in chunks],
            [pltpu.VMEM((OWN * SRC * CAPS[k], SRC * ROWS[k]), BF16) for k in chunks],
            [pltpu.VMEM((KD, OWN * SRC * CAPS[k]), BF16) for k in chunks],
            [pltpu.VMEM((OWN * SRC * CAPS[k], COLS), BF16) for k in chunks],
            [pltpu.VMEM((OWN * SRC * CAPS[k], COLS), BF16) for k in chunks],
            pltpu.SemaphoreType.DMA((2,)),
            pltpu.SemaphoreType.DMA((2, SRC)),
            pltpu.SemaphoreType.DMA((2, CHUNKS, SRC)),
            pltpu.SemaphoreType.DMA((2, CHUNKS)),
            pltpu.SemaphoreType.DMA((2, CHUNKS)),
            pltpu.SemaphoreType.DMA((2, CHUNKS, SRC)),
            pltpu.SemaphoreType.DMA((2, CHUNKS, SRC)),
            pltpu.SemaphoreType.DMA((2, OWN)),
            pltpu.SemaphoreType.DMA((2, CHUNKS, OWN)),
            pltpu.SemaphoreType.DMA((2, 2)),
        ],
        name="nystrom",
        compiler_params=pltpu.CompilerParams(
            collective_id=1, has_side_effects=True, vmem_limit_bytes=60 * 2**20
        ),
    )(
        points,
        assignments.reshape(1, PTS),
        owner_map.reshape(128, 128),
        landmarks,
        factor,
    )
    features = lax.dot_general(
        perm, sorted_features, (((0,), (0,)), ((), ())), preferred_element_type=F32
    ).astype(BF16)
    seen = seen[0][:, None]
    centroids = jnp.where(seen > 0, sums.T / jnp.maximum(seen, 1.0), old_centroids)
    return (features, centroids)


def solution(mesh):
    in_specs = (
        P(("dp", "land"), None),
        P("land", None),
        P("land", None),
        P(("dp", "land")),
        P(),
        P("dp", "land"),
    )
    out_specs = (P(("dp", "land"), None), P("dp", "land"))
    return jax.shard_map(
        per_device, mesh=mesh, in_specs=in_specs, out_specs=out_specs, check_vma=False
    )
```

time: 84.4 us -> 79.8 us (0.945); the launches traced: 84.2 us -> 78.5 us
  local copies, waits for them, and re-layouts: 4.57 us -> 0.01 us
  matrix products: 0 us -> 1.89 us
  Pallas kernels: 74.4 us -> 72.7 us
  other arithmetic: 4.51 us -> 3.23 us
    unnamed x4 -> x2, local copies, waits for them, and re-layouts: 3.42 us -> 0.01 us
    dot_general x0 -> x1, matrix products: none -> 1.89 us  [per_device(): lax.dot_general(perm, sorted_features, (((0,), (0,)), ((), ())), preferre...]
    pallas_call x1, Pallas kernels: 74.4 us -> 72.7 us  [per_device(): pl.pallas_call(functools.partial(body, sharpness), out_shape=(jax.ShapeDt...]
    reduce_sum x3 -> x0, other arithmetic: 1.26 us -> none  [the longest x1 0.91 us: per_device(): jnp.sum(jnp.where((rows % 4 == chunk) & (lanes == lane), values, 0), axis=2)]
    gather x1 -> x0, local copies, waits for them, and re-layouts: 1.15 us -> none  [per_device(): slot_ids = jnp.take(owner_map, assignments)]
where the time goes in v2:
time: 79.8 us; the launch traced here: 78.5 us
  Pallas kernels  72.7 us (91%)
  other arithmetic  3.23 us (4%)
  matrix products  1.89 us (2%)
    pallas_call x1, Pallas kernels, per_device(): pl.pallas_call(functools.partial(body, sharpness), out_shape=(jax.ShapeDt...  72.7 us
    dot_general x1, matrix products, per_device(): lax.dot_general(perm, sorted_features, (((0,), (0,)), ((), ())), preferre...  1.89 us
    select_n x1, other arithmetic, per_device(): jnp.where(seen > 0, sums.T / jnp.maximum(seen, 1.0), old_centroids)  1.69 us

profile of v2, /device:TPU:11, one launch (start us, length us, event | category | flops | bytes accessed | tf_op | source)
XLA Modules:
  0.0 78.5 jit_solution(14797777396932597203)
XLA Ops:
  0.6 0.0 copy-start
  0.6 72.7 %nystrom.1 = (bf16[112,1024]{1,0:T(8,128)(2,1)}, bf16[112,112]{1,0:T(8,128)(2,1)}, f32[64,1024]{1,0:T(8,128)}, f32[8,1024]{1,0:T(8,128)}) custom-call(bf16[112,768]{1,0:T(8,128)(2,1)} %points_ref.1, s32[1,112]{1,0:T(1,128)} %bitcast.9, s32[128,128]{1,0:T(8,128)} %bitcast.7, bf16[2048,768]{1,0:T(8,128)(2,1)} %land_ref.1, bf16[2048,1024]{1,0:T(8,128)(2,1)} %factor_ref.1), custom_call_target="tpu_custom_call" | custom-call | tf_op jit(solution)/shard_map/nystrom/pallas_call | solution.py:489
  73.4 1.9 %convolution_convert_fusion = bf16[112,1024]{1,0:T(8,128)(2,1)} fusion(bf16[112,112]{1,0:T(8,128)(2,1)} %get-tuple-element.6, bf16[112,1024]{1,0:T(8,128)(2,1)} %get-tuple-element.7), kind=kOutput, calls=%fused_computation | convolution fusion | flops 25804800 | bytes 483840 | tf_op jit(solution)/shard_map/dot_general | solution.py:543
  75.3 0.8 compare_reduce_fusion
  76.0 0.8 slice_maximum_fusion
  76.8 0.0 copy-done
  76.8 1.7 %bitcast_select_fusion = f32[1024,64]{0,1:T(8,128)} fusion(f32[1024,64]{0,1:T(8,128)S(1)} %copy-done, f32[64,1024]{1,0:T(8,128)} %get-tuple-element.9, f32[1024]{0:T(1024)S(1)} %bitcast.8, pred[1024]{0:T(1024)(128)(4,1)S(1)} %compare_reduce_fusion), kind=kLoop, calls=%fused_computation.1 | loop fusion | flops 131072 | bytes 791552 | tf_op jit(solution)/shard_map/jit(_where)/select_n | solution.py:547
Async XLA Ops:
  0.6 76.2 %copy-start = (f32[1024,64]{0,1:T(8,128)S(1)}, f32[1024,64]{0,1:T(8,128)}, u32[]{:S(2)}) copy-start(f32[1024,64]{0,1:T(8,128)} %param.11) | copy-start | bytes 786436
